TPU v7x, 128 devices: a whole 4x4x4 slice. The times are simulated.
128 devices in a mesh: gr: 8 (over y_hi, z), gc: 16 (over x, y_lo, core).
Axes of the slice: x: 4, y: 4 (y_hi: 2, y_lo: 2; y = y_hi * 2 + y_lo), z: 4, core: 2. Of those that a mesh axis runs over, the one named last changes fastest.
Arguments:
- items: bfloat16 [16384, 4096], P(('gr', 'gc'))
- position_of: int32 [16384], P(('gr', 'gc')), may hold values from 0 to 16383, as said below
Outputs:
- similarity: bfloat16 [16384, 16384], P('gr', 'gc')
- best_other: float32 [16384], P('gr')
Inputs may be any that keep to these rules, and one draw needn't show every extreme that they name: `position_of`: A permutation. Position p has home device p // 128 in the order gr+gc; the items of device s go to home devices s * 128, s * 128 + 1, ... taken modulo 128, so each device sends at most 1 items to each home device and each home device receives 128.
All inputs are finite; a program needn't handle non-finite values.
Results may differ from a plain program's by a relative error of at most 0.001.
Values may be sent and summed in bfloat16 or wider, within the bound.
No kernel may reach another device: no remote copies, remote signals or barrier semaphores. Data moves between devices by JAX's collectives and lax.ppermute only.
A program may use at most 128 MiB of HBM per device.

v0:
```python
import jax
import jax.numpy as jnp
from jax import lax
from jax.sharding import PartitionSpec as P


def inverse_norm(block):
    wide = block.astype(jnp.float32)
    return 1.0 / jnp.sqrt(jnp.sum(wide * wide, axis=1) + 1e-06)


def per_device(items, position_of):
    count = items.shape[0]
    width = items.shape[1]
    n_rows = lax.axis_size("gr")
    n_cols = lax.axis_size("gc")
    shards = n_rows * n_cols
    slots = (count + shards - 1) // shards
    dest = position_of // count
    earlier = (dest[None, :] == dest[:, None]) & (position_of[None, :] < position_of[:, None])
    rank = jnp.sum(earlier.astype(jnp.int32), axis=1)
    slot = dest * slots + rank
    send = jnp.zeros((shards * slots, width), items.dtype).at[slot].set(items)
    send_pos = jnp.full((shards * slots,), -1, jnp.int32).at[slot].set(position_of)
    arrived, arrived_pos = (
        lax.all_to_all(send, ("gr", "gc"), split_axis=0, concat_axis=0, tiled=True),
        lax.all_to_all(send_pos, ("gr", "gc"), split_axis=0, concat_axis=0, tiled=True),
    )
    target = jnp.where(arrived_pos >= 0, arrived_pos % count, count)
    local = jnp.zeros_like(items).at[target].set(arrived, mode="drop")
    rows = lax.all_gather(local, "gc", axis=0, tiled=True)
    row_inv = inverse_norm(rows)
    piece = lax.all_gather(local, "gr", axis=0, tiled=True)
    product = lax.dot_general(
        rows, piece, (((1,), (1,)), ((), ())), preferred_element_type=jnp.float32
    )
    scaled = product * row_inv[:, None] * inverse_norm(piece)[None, :]
    row_here = lax.axis_index("gr")
    col_here = lax.axis_index("gc")
    row_local = jnp.arange(count * n_cols, dtype=jnp.int32)[:, None]
    col_local = jnp.arange(count * n_rows, dtype=jnp.int32)[None, :]
    itself = (row_local == col_here * count + col_local % count) & (col_local // count == row_here)
    masked = jnp.where(itself, jnp.float32(-2.0), scaled)
    best = lax.pmax(jnp.max(masked, axis=1), "gc")
    return (scaled.astype(jnp.bfloat16), best)


def solution(mesh):
    return jax.shard_map(
        per_device,
        mesh=mesh,
        in_specs=(P(("gr", "gc"), None), P(("gr", "gc"))),
        out_specs=(P("gr", "gc"), P("gr")),
        check_vma=False,
    )
```

profile of v0, /device:TPU:0, one launch (start us, length us, event | category | flops | bytes accessed | tf_op | source)
XLA Modules:
  0.0 335.4 jit_solution(11335868931634280589)
XLA Ops:
  7.2 0.7 and_select_fusion.1
  7.8 0.9 convert_reduce_fusion
  8.7 0.7 compare_select_fusion.1
  9.4 1.1 scatter_custom_fusion
  10.5 0.7 copy.12
  11.3 11.1 %all-to-all-start = ((s32[128,1,1]{2,1,0:T(1,128)}), s32[128,1,1]{2,1,0:T(1,128)S(1)}, u32[]{:S(2)}, u32[]{:S(2)}) async-start(s32[128,1,1]{2,1,0:T(1,128)} %copy.12), calls=%async_computation | async-start | bytes 131072 | tf_op jit(solution)/shard_map/all_to_all | solution.py:27
  22.4 3.0 scatter_custom_fusion.1
  25.4 0.5 broadcast.174
  25.9 1.4 reduce.1
  27.3 1.6 reshape.182
  28.9 2.7 all-to-all-done
  31.6 7.1 %all-to-all-start.1 = ((bf16[128,2,2048]{2,1,0:T(2,128)(2,1)}), bf16[128,2,2048]{2,1,0:T(2,128)(2,1)S(1)}, u32[]{:S(2)}, u32[]{:S(2)}) async-start(bf16[128,2,2048]{2,1,0:T(2,128)(2,1)} %reshape.182), calls=%async_computation.1 | async-start | bytes 2097152 | tf_op jit(solution)/shard_map/all_to_all | solution.py:26
  38.7 0.0 all-gather.5.cloned.1.call-start
  38.7 2.4 reduce
  41.1 16.5 %all-to-all-done.1 = bf16[128,2,2048]{2,1,0:T(2,128)(2,1)S(1)} async-done(((bf16[128,2,2048]{2,1,0:T(2,128)(2,1)}), bf16[128,2,2048]{2,1,0:T(2,128)(2,1)S(1)}, u32[]{:S(2)}, u32[]{:S(2)}) %all-to-all-start.1) | async-done | bytes 1048608 | tf_op jit(solution)/shard_map/all_to_all | solution.py:26
  57.6 1.0 reshape.183
  58.7 4.1 %scatter_custom_fusion.2 = bf16[128,4096]{1,0:T(8,128)(2,1)} fusion(s32[128]{0:T(128)S(1)} %fusion.16, bf16[128,1,4096]{2,1,0:T(2,128)(2,1)S(1)} %reshape.183, bf16[]{:T(256)} %constant.60.clone.1), kind=kCustom, calls=%fused_computation.10 | custom fusion | bytes 3145730 | tf_op jit(solution)/shard_map/scatter | solution.py:30
  62.8 0.0 all-gather.5.cloned.1.call-update
  62.8 0.2 all-gather.3.cloned.1.call-start
  63.0 0.5 all-gather.3.cloned.1.call-update
  63.6 103.0 %all-gather.5.cloned.1.call-done = bf16[1024,4096]{1,0:T(8,128)(2,1)} async-done(((bf16[128,4096]{1,0:T(8,128)(2,1)}), bf16[1024,4096]{1,0:T(8,128)(2,1)}) %all-gather.5.cloned.1.call-update) | async-done | bytes 8388624 | tf_op jit(solution)/shard_map/all_gather | solution.py:33
  166.6 5.1 %multiply_reduce_fusion.1 = f32[1024]{0:T(1024)S(1)} fusion(bf16[1024,4096]{1,0:T(8,128)(2,1)} %all-gather.5.cloned.1.call-done), kind=kLoop, calls=%fused_computation.4 | loop fusion | flops 12581888 | bytes 8392704 | tf_op jit(solution)/shard_map/reduce_sum | solution.py:9
  171.7 86.5 %all-gather.3.cloned.1.call-done = bf16[2048,4096]{1,0:T(8,128)(2,1)} async-done(((bf16[128,4096]{1,0:T(8,128)(2,1)}), bf16[2048,4096]{1,0:T(8,128)(2,1)}) %all-gather.3.cloned.1.call-update) | async-done | bytes 16777232 | tf_op jit(solution)/shard_map/all_gather | solution.py:31
  258.2 0.0 copy-start
  258.2 7.5 %multiply_reduce_fusion = f32[2048]{0:T(1024)S(1)} fusion(bf16[2048,4096]{1,0:T(8,128)(2,1)} %all-gather.3.cloned.1.call-done), kind=kLoop, calls=%fused_computation.3 | loop fusion | flops 25163776 | bytes 16785408 | tf_op jit(solution)/shard_map/reduce_sum | solution.py:9
  265.7 3.1 copy-done
  268.8 22.5 %select_reduce_fusion = (f32[2048]{0:T(1024)S(1)}, bf16[2048,1024]{0,1:T(8,128)(2,1)}) fusion(s32[1024]{0:T(1024)S(1)} %fusion.8, f32[1024]{0:T(1024)S(1)} %add_rsqrt_fusion.1, f32[2048]{0:T(1024)S(1)} %add_rsqrt_fusion, pred[1024]{0:T(1024)(128)(4,1)S(1)} %fusion.10, bf16[2048,4096]{1,0:T(8,128)(2,1)S(1)} %copy-done, ...), kind=kOutput, calls=%fused_computation.5 | convolution fusion | flops 17194547200 | bytes 29385728 | tf_op jit(solution)/shard_map/dot_general | solution.py:34
  291.3 30.9 %pmax.7 = f32[2048]{0:T(1024)} all-reduce(f32[2048]{0:T(1024)S(1)} %get-tuple-element.12), channel_id=1, replica_groups=mesh['gr'=8,'gc'=16] {'gc'}, use_global_device_ids=true, to_apply=%region_7.8 | all-reduce | flops 2048 | bytes 16384 | tf_op jit(solution)/shard_map/pmax | solution.py:44
  322.2 6.4 %copy.14 = bf16[2048,1024]{1,0:T(8,128)(2,1)} copy(bf16[2048,1024]{0,1:T(8,128)(2,1)} %get-tuple-element.13) | data formatting | bytes 8388608
  (5 shorter events, 0.0 us)
Async XLA Ops:
  11.3 20.3 %all-to-all-start = ((s32[128,1,1]{2,1,0:T(1,128)}), s32[128,1,1]{2,1,0:T(1,128)S(1)}, u32[]{:S(2)}, u32[]{:S(2)}) async-start(s32[128,1,1]{2,1,0:T(1,128)} %copy.12), calls=%async_computation | async-start | bytes 131072 | tf_op jit(solution)/shard_map/all_to_all | solution.py:27
  31.6 26.0 %all-to-all-start.1 = ((bf16[128,2,2048]{2,1,0:T(2,128)(2,1)}), bf16[128,2,2048]{2,1,0:T(2,128)(2,1)S(1)}, u32[]{:S(2)}, u32[]{:S(2)}) async-start(bf16[128,2,2048]{2,1,0:T(2,128)(2,1)} %reshape.182), calls=%async_computation.1 | async-start | bytes 2097152 | tf_op jit(solution)/shard_map/all_to_all | solution.py:26
  38.7 127.9 %all-gather.5.cloned.1.call-start = ((), (), s32[]{:S(2)}) async-start(), calls=%async_computation.3 | async-start | bytes 9437184 | tf_op jit(solution)/shard_map/all_gather | solution.py:33
  62.8 195.4 %all-gather.3.cloned.1.call-start = ((), (), s32[]{:S(2)}) async-start(), calls=%async_computation.2 | async-start | bytes 17825792 | tf_op jit(solution)/shard_map/all_gather | solution.py:31
  258.2 10.7 %copy-start = (bf16[2048,4096]{1,0:T(8,128)(2,1)S(1)}, bf16[2048,4096]{1,0:T(8,128)(2,1)}, u32[]{:S(2)}) copy-start(bf16[2048,4096]{1,0:T(8,128)(2,1)} %all-gather.3.cloned.1.call-done) | copy-start | bytes 50331652
Sparse Core Ops, SparseCore 0:
  62.9 103.5 all-gather.4
  168.8 89.2 all-gather.2
where the time goes:
time: 336 us; the launch traced here: 335 us
  waiting for transfers between devices  209 us (62%)
  blocking collectives  30.9 us (9%)
  matrix products  22.5 us (7%)
  local copies, waits for them, and re-layouts  21.6 us (6%)
  other arithmetic  18.6 us (6%)
  starting transfers between devices  18.5 us (6%)
  between operations  14.1 us (4%)
    all_gather x1, waiting for transfers between devices, per_device(): piece = lax.all_gather(local, 'gr', axis=0, tiled=True)  103 us
    all_gather x1, waiting for transfers between devices, per_device(): rows = lax.all_gather(local, 'gc', axis=0, tiled=True)  86.5 us
    pmax x1, blocking collectives, per_device(): best = lax.pmax(jnp.max(masked, axis=1), 'gc')  30.9 us
    dot_general x1, matrix products, per_device(): lax.dot_general(rows, piece, (((1,), (1,)), ((), ())), preferred_element_...  22.5 us
    all_to_all x1, waiting for transfers between devices, per_device(): lax.all_to_all(send, ('gr', 'gc'), split_axis=0, concat_axis=0, tiled=True)  16.5 us
    reduce_sum x2, other arithmetic, inverse_norm(): return 1.0 / jnp.sqrt(jnp.sum(wide * wide, axis=1) + 1e-06)  12.6 us
    unnamed x5, local copies, waits for them, and re-layouts  12.1 us
    all_to_all x1, starting transfers between devices, per_device(): lax.all_to_all(send_pos, ('gr', 'gc'), split_axis=0, concat_axis=0, tiled...  11.1 us
  transfers between devices with their start and end apart: 4, of which 4 were waited for; matrix products, arithmetic and copies ran while one was open for 4% of the time, Pallas kernels for 0%

commit v1 on v0

--- a/solution.py
+++ b/solution.py
@@ -28,7 +28,9 @@
     )
     target = jnp.where(arrived_pos >= 0, arrived_pos % count, count)
     local = jnp.zeros_like(items).at[target].set(arrived, mode="drop")
-    rows = lax.all_gather(local, "gc", axis=0, tiled=True)
+    rows = jnp.concatenate(
+        lax.all_to_all(jnp.stack([local] * lax.axis_size("gc")), "gc", 0, 0), axis=0
+    )
     row_inv = inverse_norm(rows)
     piece = lax.all_gather(local, "gr", axis=0, tiled=True)
     product = lax.dot_general(

time: 336 us -> 420 us (1.25)
  waiting for transfers between devices: 209 us -> 286 us
  starting transfers between devices: 18.5 us -> 23.6 us
    all_gather x1, waiting for transfers between devices: 103 us -> 208 us  [per_device(): piece = lax.all_gather(local, 'gr', axis=0, tiled=True)]
    all_gather x1 -> x0, waiting for transfers between devices: 86.5 us -> none  [per_device(): rows = lax.all_gather(local, 'gc', axis=0, tiled=True)]
    all_to_all x0 -> x1, waiting for transfers between devices: none -> 57.5 us  [per_device(): lax.all_to_all(jnp.stack([local] * lax.axis_size('gc')), 'gc', 0, 0)]
    another operation x0 -> x1, local copies, waits for them, and re-layouts: none -> 6.17 us  [per_device(): jnp.stack([local] * lax.axis_size('gc'))]
    all_to_all x0 -> x1, starting transfers between devices: none -> 5.16 us  [per_device(): lax.all_to_all(jnp.stack([local] * lax.axis_size('gc')), 'gc', 0, 0)]
  transfers between devices with their start and end apart: 4 -> 4, of which waited for: 4 -> 4; matrix products, arithmetic and copies ran while one was open for 4% -> 3% of each run, Pallas kernels for 0% -> 0%
where the time goes in v1:
time: 420 us; the launch traced here: 419 us
  waiting for transfers between devices  286 us (68%)
  blocking collectives  28.2 us (7%)
  matrix products  25.1 us (6%)
  local copies, waits for them, and re-layouts  23.9 us (6%)
  starting transfers between devices  23.6 us (6%)
  other arithmetic  18.3 us (4%)
  between operations  14.1 us (3%)
    all_gather x1, waiting for transfers between devices, per_device(): piece = lax.all_gather(local, 'gr', axis=0, tiled=True)  208 us
    all_to_all x1, waiting for transfers between devices, per_device(): lax.all_to_all(jnp.stack([local] * lax.axis_size('gc')), 'gc', 0, 0)  57.5 us
    pmax x1, blocking collectives, per_device(): best = lax.pmax(jnp.max(masked, axis=1), 'gc')  28.2 us
    dot_general x1, matrix products, per_device(): lax.dot_general(rows, piece, (((1,), (1,)), ((), ())), preferred_element_...  25.1 us
    all_to_all x1, waiting for transfers between devices, per_device(): lax.all_to_all(send, ('gr', 'gc'), split_axis=0, concat_axis=0, tiled=True)  16.6 us
    reduce_sum x2, other arithmetic, inverse_norm(): return 1.0 / jnp.sqrt(jnp.sum(wide * wide, axis=1) + 1e-06)  12.3 us
    all_to_all x1, starting transfers between devices, per_device(): lax.all_to_all(send_pos, ('gr', 'gc'), split_axis=0, concat_axis=0, tiled...  11.1 us
    unnamed x5, local copies, waits for them, and re-layouts  9.03 us
  transfers between devices with their start and end apart: 4, of which 4 were waited for; matrix products, arithmetic and copies ran while one was open for 3% of the time, Pallas kernels for 0%

profile of v1, /device:TPU:0, one launch (start us, length us, event | category | flops | bytes accessed | tf_op | source)
XLA Modules:
  0.0 418.8 jit_solution(4130195910709178444)
XLA Ops:
  7.2 0.7 and_select_fusion.1
  7.8 0.9 convert_reduce_fusion
  8.7 0.7 compare_select_fusion.1
  9.4 1.1 scatter_custom_fusion
  10.5 0.7 copy.12
  11.3 11.1 %all-to-all-start = ((s32[128,1,1]{2,1,0:T(1,128)}), s32[128,1,1]{2,1,0:T(1,128)S(1)}, u32[]{:S(2)}, u32[]{:S(2)}) async-start(s32[128,1,1]{2,1,0:T(1,128)} %copy.12), calls=%async_computation | async-start | bytes 131072 | tf_op jit(solution)/shard_map/all_to_all | solution.py:27
  22.4 3.0 scatter_custom_fusion.1
  25.4 0.5 broadcast.178
  25.9 1.4 reduce.2
  27.3 1.6 reshape.195
  28.9 2.7 all-to-all-done
  31.6 7.1 %all-to-all-start.1 = ((bf16[128,2,2048]{2,1,0:T(2,128)(2,1)}), bf16[128,2,2048]{2,1,0:T(2,128)(2,1)S(1)}, u32[]{:S(2)}, u32[]{:S(2)}) async-start(bf16[128,2,2048]{2,1,0:T(2,128)(2,1)} %reshape.195), calls=%async_computation.1 | async-start | bytes 2097152 | tf_op jit(solution)/shard_map/all_to_all | solution.py:26
  38.7 2.4 reduce.1
  41.1 16.6 %all-to-all-done.1 = bf16[128,2,2048]{2,1,0:T(2,128)(2,1)S(1)} async-done(((bf16[128,2,2048]{2,1,0:T(2,128)(2,1)}), bf16[128,2,2048]{2,1,0:T(2,128)(2,1)S(1)}, u32[]{:S(2)}, u32[]{:S(2)}) %all-to-all-start.1) | async-done | bytes 1048608 | tf_op jit(solution)/shard_map/all_to_all | solution.py:26
  57.6 1.0 reshape.196
  58.7 3.4 scatter_custom_fusion.2
  62.1 0.0 copy-start
  62.1 6.2 %stack.2 = bf16[16,128,4096]{2,1,0:T(8,128)(2,1)} broadcast(bf16[128,4096]{1,0:T(8,128)(2,1)S(1)} %scatter_custom_fusion.2), dimensions={1,2} | broadcast | bytes 17825792 | tf_op jit(solution)/shard_map/stack | solution.py:32
  68.2 0.0 copy-done
  68.2 5.2 %all-to-all-start.2 = ((bf16[16,128,4096]{2,1,0:T(8,128)(2,1)}), bf16[16,128,4096]{2,1,0:T(8,128)(2,1)}, u32[]{:S(2)}, u32[]{:S(2)}) async-start(bf16[16,128,4096]{2,1,0:T(8,128)(2,1)} %stack.2), calls=%async_computation.2 | async-start | bytes 33554432 | tf_op jit(solution)/shard_map/all_to_all | solution.py:32
  73.4 0.2 all-gather.2.cloned.1.call-start
  73.6 0.5 all-gather.2.cloned.1.call-update
  74.2 208.2 %all-gather.2.cloned.1.call-done = bf16[1024,4096]{1,0:T(8,128)(2,1)} async-done(((bf16[128,4096]{1,0:T(8,128)(2,1)}), bf16[1024,4096]{1,0:T(8,128)(2,1)}) %all-gather.2.cloned.1.call-update) | async-done | bytes 8388624 | tf_op jit(solution)/shard_map/all_gather | solution.py:35
  282.4 5.1 %multiply_reduce_fusion.1 = f32[1024]{0:T(1024)S(1)} fusion(bf16[1024,4096]{1,0:T(8,128)(2,1)} %all-gather.2.cloned.1.call-done), kind=kLoop, calls=%fused_computation.4 | loop fusion | flops 12581888 | bytes 8392704 | tf_op jit(solution)/shard_map/reduce_sum | solution.py:9
  287.5 57.5 %all-to-all-done.2 = bf16[16,128,4096]{2,1,0:T(8,128)(2,1)} async-done(((bf16[16,128,4096]{2,1,0:T(8,128)(2,1)}), bf16[16,128,4096]{2,1,0:T(8,128)(2,1)}, u32[]{:S(2)}, u32[]{:S(2)}) %all-to-all-start.2) | async-done | bytes 16777248 | tf_op jit(solution)/shard_map/all_to_all | solution.py:32
  345.0 7.2 %multiply_reduce_fusion = f32[16,128]{1,0:T(8,128)S(1)} fusion(bf16[16,128,4096]{2,1,0:T(8,128)(2,1)} %all-to-all-done.2), kind=kLoop, calls=%fused_computation.3 | loop fusion | flops 25163776 | bytes 16785408 | tf_op jit(solution)/shard_map/reduce_sum | solution.py:9
  352.2 25.1 %select_reduce_fusion = (f32[2048]{0:T(1024)S(1)}, bf16[2048,1024]{0,1:T(8,128)(2,1)}) fusion(s32[1024]{0:T(1024)S(1)} %fusion.8, f32[1024]{0:T(1024)S(1)} %add_rsqrt_fusion, f32[2048]{0:T(1024)S(1)} %rsqrt_bitcast_fusion, pred[1024]{0:T(1024)(128)(4,1)S(1)} %fusion.10, bf16[2048,4096]{1,0:T(8,128)(2,1)} %bitcast.3, ...), kind=kOutput, calls=%fused_computation.5 | convolution fusion | flops 17194547200 | bytes 29385728 | tf_op jit(solution)/shard_map/dot_general | solution.py:36
  377.3 6.4 %copy.14 = bf16[2048,1024]{1,0:T(8,128)(2,1)} copy(bf16[2048,1024]{0,1:T(8,128)(2,1)} %get-tuple-element.13) | data formatting | bytes 8388608
  383.7 28.2 %pmax.7 = f32[2048]{0:T(1024)} all-reduce(f32[2048]{0:T(1024)S(1)} %get-tuple-element.12), channel_id=1, replica_groups=mesh['gr'=8,'gc'=16] {'gc'}, use_global_device_ids=true, to_apply=%region_7.8 | all-reduce | flops 2048 | bytes 16384 | tf_op jit(solution)/shard_map/pmax | solution.py:46
  (5 shorter events, 0.0 us)
Async XLA Ops:
  11.3 20.3 %all-to-all-start = ((s32[128,1,1]{2,1,0:T(1,128)}), s32[128,1,1]{2,1,0:T(1,128)S(1)}, u32[]{:S(2)}, u32[]{:S(2)}) async-start(s32[128,1,1]{2,1,0:T(1,128)} %copy.12), calls=%async_computation | async-start | bytes 131072 | tf_op jit(solution)/shard_map/all_to_all | solution.py:27
  31.6 26.0 %all-to-all-start.1 = ((bf16[128,2,2048]{2,1,0:T(2,128)(2,1)}), bf16[128,2,2048]{2,1,0:T(2,128)(2,1)S(1)}, u32[]{:S(2)}, u32[]{:S(2)}) async-start(bf16[128,2,2048]{2,1,0:T(2,128)(2,1)} %reshape.195), calls=%async_computation.1 | async-start | bytes 2097152 | tf_op jit(solution)/shard_map/all_to_all | solution.py:26
  62.1 6.2 %copy-start = (bf16[128,4096]{1,0:T(8,128)(2,1)}, bf16[128,4096]{1,0:T(8,128)(2,1)S(1)}, u32[]{:S(2)}) copy-start(bf16[128,4096]{1,0:T(8,128)(2,1)S(1)} %scatter_custom_fusion.2) | copy-start | bytes 3145732
  68.2 276.8 %all-to-all-start.2 = ((bf16[16,128,4096]{2,1,0:T(8,128)(2,1)}), bf16[16,128,4096]{2,1,0:T(8,128)(2,1)}, u32[]{:S(2)}, u32[]{:S(2)}) async-start(bf16[16,128,4096]{2,1,0:T(8,128)(2,1)} %stack.2), calls=%async_computation.2 | async-start | bytes 33554432 | tf_op jit(solution)/shard_map/all_to_all | solution.py:32
  73.4 209.0 %all-gather.2.cloned.1.call-start = ((), (), s32[]{:S(2)}) async-start(), calls=%async_computation.3 | async-start | bytes 9437184 | tf_op jit(solution)/shard_map/all_gather | solution.py:35
Sparse Core Ops, SparseCore 0:
  77.2 205.1 all-gather.1
